TPU v7x, 32 devices: a whole 2x2x4 slice. The times are simulated.
32 devices in a mesh: grp: 2 (over x), dp: 16 (over z, y, core).
Axes of the slice: x: 2, y: 2, z: 4, core: 2. Of those that a mesh axis runs over, the one named last changes fastest.
Arguments:
- inputs: bfloat16 [8192, 8192], P('grp', 'dp'), parts along dimension 0, may hold values from -6 to 6
- out_grads: bfloat16 [8192, 28672], P('grp', 'dp'), parts along dimension 0, may hold values from -6 to 6
- in_basis: bfloat16 [8192, 64], P('dp'), may hold values from -0.0625 to 0.0625
- out_basis: bfloat16 [28672, 64], P('dp'), may hold values from -0.03125 to 0.03125
- example_ids: int32 [32, 256], P(('grp', 'dp')), parts along dimension 0, may hold values from 0 to 15, never falling along the last dimension, each value on 1 to 32 neighbouring positions
- loss_counts: int32 [32, 16], P(('grp', 'dp')), parts along dimension 0, may hold values from 1 to 32
- queries: bfloat16 [2048, 4096], P('dp'), may hold values from -0.09375 to 0.09375
Outputs:
- scores: float32 [512, 2048], P(('grp', 'dp')), parts along dimension 0
There are 2 independent parts, one for each index of `grp`. A program takes and returns all parts, laid end to end along the dimension named above; an argument that names none is the same for every part. Nothing has to cross between parts.
Inputs may be any that keep to these rules, and one draw needn't show every extreme that they name: `example_ids`: each row lists the examples of one device's tokens, never falling, every example 1 to 32 tokens, one exactly 32.
All inputs are finite; a program needn't handle non-finite values.
Results may differ from a plain program's by a relative error of at most 0.0049.
Values may be sent and summed in bfloat16 or wider, within the bound.
A program may use at most 128 MiB of HBM per device.

v0:
```python
import jax
import jax.numpy as jnp
from jax import lax
from jax.sharding import PartitionSpec as P


def local(inputs, out_grads, in_basis, out_basis, example_ids, loss_counts, queries):
    tok_rows = example_ids.shape[1]
    example_count = loss_counts.shape[1]
    rank_size = in_basis.shape[1]
    left = jnp.dot(inputs, in_basis, preferred_element_type=jnp.float32)
    right = jnp.dot(out_grads, out_basis, preferred_element_type=jnp.float32)
    totals = lax.psum(jnp.concatenate([left, right], axis=1), "dp")
    mine = lax.dynamic_slice_in_dim(totals, lax.axis_index("dp") * tok_rows, tok_rows, 0)
    in_low = lax.optimization_barrier(mine[:, :rank_size].astype(jnp.bfloat16)).astype(jnp.float32)
    out_low = lax.optimization_barrier(mine[:, rank_size:].astype(jnp.bfloat16)).astype(jnp.float32)
    labels = jnp.arange(example_count, dtype=jnp.int32)
    onehot = (example_ids[0][None, :] == labels[:, None]).astype(jnp.float32)
    grads = jnp.einsum("et,ti,to->eio", onehot, in_low, out_low)
    grads = grads / loss_counts[0].astype(jnp.float32)[:, None, None]
    flat = grads.reshape(example_count, rank_size * rank_size).astype(jnp.bfloat16)
    return lax.dot_general(
        flat,
        lax.all_gather(queries, "dp", axis=0, tiled=True),
        (((1,), (1,)), ((), ())),
        preferred_element_type=jnp.float32,
    )


def solution(mesh):
    in_specs = (
        P("grp", "dp"),
        P("grp", "dp"),
        P("dp", None),
        P("dp", None),
        P(("grp", "dp"), None),
        P(("grp", "dp"), None),
        P("dp", None),
    )
    out_specs = P(("grp", "dp"), None)
    return jax.shard_map(local, mesh=mesh, in_specs=in_specs, out_specs=out_specs, check_vma=False)
```

profile of v0, /device:TPU:0, one launch (start us, length us, event | category | flops | bytes accessed | tf_op | source)
XLA Modules:
  0.0 186.0 jit_solution(3239193753779713365)
XLA Ops:
  6.5 0.0 copy-start
  6.5 0.0 all-gather.2.cloned.1.call-start
  6.5 0.7 all-gather.2.cloned.1.call-update
  7.3 0.0 copy-start.2
  7.3 0.0 copy-start.1
  7.3 3.6 %fusion.7 = f32[4096,64]{0,1:T(8,128)S(1)} fusion(bf16[4096,512]{1,0:T(8,128)(2,1)} %param.7, bf16[512,64]{0,1:T(8,128)(2,1)} %param.9), kind=kOutput, calls=%fused_computation.13 | convolution fusion | flops 268435456 | bytes 5308416 | tf_op jit(solution)/shard_map/dot_general | solution.py:11
  10.9 0.0 copy-done
  10.9 9.7 %fusion.8 = f32[4096,64]{0,1:T(8,128)S(1)} fusion(bf16[4096,1792]{1,0:T(8,128)(2,1)} %param.8, bf16[1792,64]{0,1:T(8,128)(2,1)S(1)} %copy-done), kind=kOutput, calls=%fused_computation.14 | convolution fusion | flops 939524096 | bytes 15958016 | tf_op jit(solution)/shard_map/dot_general | solution.py:12
  20.5 0.2 pad_maximum_fusion
  20.7 98.4 %all-reduce.1 = bf16[4096,128]{0,1:T(8,128)(2,1)S(1)} all-reduce(f32[4096,128]{0,1:T(8,128)S(1)} %pad_maximum_fusion), channel_id=1, replica_groups=mesh['grp'=2,'dp'=16] {'dp'}, use_global_device_ids=true, to_apply=%region_0.0 | all-reduce | flops 524288 | bytes 3145728 | tf_op jit(solution)/shard_map/psum | solution.py:13
  119.2 0.0 copy-done.2
  119.2 0.0 copy-done.1
  119.2 0.3 fusion.1
  119.5 0.1 copy.8
  119.6 0.3 convert_element_type.28
  119.9 48.4 %all-gather.2.cloned.1.call-done = bf16[2048,4096]{1,0:T(8,128)(2,1)} async-done(((bf16[128,4096]{1,0:T(8,128)(2,1)}), bf16[2048,4096]{1,0:T(8,128)(2,1)}) %all-gather.2.cloned.1.call-update) | async-done | bytes 16777232 | tf_op jit(solution)/shard_map/all_gather | solution.py:24
  168.2 10.9 %fusion.9 = f32[16,2048]{1,0:T(8,128)} fusion(bf16[16,4096]{1,0:T(8,128)(2,1)S(1)} %convert_element_type.28, bf16[2048,4096]{1,0:T(8,128)(2,1)} %all-gather.2.cloned.1.call-done), kind=kOutput, calls=%fused_computation.15 | convolution fusion | flops 268435456 | bytes 17039360 | tf_op jit(solution)/shard_map/dot_general | solution.py:22
  (5 shorter events, 0.0 us)
Async XLA Ops:
  6.5 4.3 %copy-start = (bf16[1792,64]{0,1:T(8,128)(2,1)S(1)}, bf16[1792,64]{0,1:T(8,128)(2,1)}, u32[]{:S(2)}) copy-start(bf16[1792,64]{0,1:T(8,128)(2,1)} %param.10) | copy-start | bytes 688132
  6.5 161.7 %all-gather.2.cloned.1.call-start = ((), (), s32[]{:S(2)}) async-start(), calls=%async_computation | async-start | bytes 17825792 | tf_op jit(solution)/shard_map/all_gather | solution.py:24
  7.3 111.9 %copy-start.2 = (s32[1,16]{1,0:T(1,128)S(1)}, s32[1,16]{1,0:T(1,128)}, u32[]{:S(2)}) copy-start(s32[1,16]{1,0:T(1,128)} %param.12) | copy-start | bytes 196
  7.3 111.9 %copy-start.1 = (s32[1,256]{1,0:T(1,128)S(1)}, s32[1,256]{1,0:T(1,128)}, u32[]{:S(2)}) copy-start(s32[1,256]{1,0:T(1,128)} %param.11) | copy-start | bytes 3076
Sparse Core Ops, SparseCore 0:
  9.5 158.6 all-gather.1
where the time goes:
time: 186 us
  blocking collectives  98.4 us (53%)
  waiting for transfers between devices  49.1 us (26%)
  matrix products  24.4 us (13%)
  between operations  13.5 us (7%)
    psum x1, blocking collectives, local(): totals = lax.psum(jnp.concatenate([left, right], axis=1), 'dp')  98.4 us
    all_gather x1, waiting for transfers between devices, local(): lax.all_gather(queries, 'dp', axis=0, tiled=True)  48.4 us
    dot_general x1, matrix products, local(): lax.dot_general(flat, lax.all_gather(queries, 'dp', axis=0, tiled=True),...  10.9 us
    dot_general x1, matrix products, local(): right = jnp.dot(out_grads, out_basis, preferred_element_type=jnp.float32)  9.67 us
  transfers between devices with their start and end apart: 1, of which 1 were waited for; matrix products, arithmetic and copies ran while one was open for 8% of the time, Pallas kernels for 0%

commit v1 on v0

v1 whole, which is shorter than its diff:
```python
import jax
import jax.numpy as jnp
from jax import lax
from jax.sharding import PartitionSpec as P


def local(inputs, out_grads, in_basis, out_basis, example_ids, loss_counts, queries):
    tok_rows = example_ids.shape[1]
    example_count = loss_counts.shape[1]
    rank_size = in_basis.shape[1]
    parts = inputs.shape[0] // tok_rows
    left = jnp.dot(inputs, in_basis, preferred_element_type=jnp.float32)
    right = jnp.dot(out_grads, out_basis, preferred_element_type=jnp.float32)
    mine = lax.psum_scatter(jnp.concatenate([left, right], axis=1), "dp", scatter_dimension=0, tiled=True)
    low = lax.optimization_barrier(mine.astype(jnp.bfloat16)).astype(jnp.float32)
    labels = jnp.arange(example_count, dtype=jnp.int32)
    onehot = (example_ids[0][None, :] == labels[:, None]).astype(jnp.float32)
    grads = jnp.einsum("et,ti,to->eio", onehot, low[:, :rank_size], low[:, rank_size:])
    grads = grads / loss_counts[0].astype(jnp.float32)[:, None, None]
    flat = grads.reshape(example_count, rank_size * rank_size).astype(jnp.bfloat16)
    every = lax.all_gather(flat, "dp", axis=0, tiled=True)
    part = lax.dot_general(every, queries, (((1,), (1,)), ((), ())), preferred_element_type=jnp.float32)
    return lax.all_to_all(part, "dp", split_axis=0, concat_axis=1, tiled=True)


def solution(mesh):
    in_specs = (
        P("grp", "dp"),
        P("grp", "dp"),
        P("dp", None),
        P("dp", None),
        P(("grp", "dp"), None),
        P(("grp", "dp"), None),
        P("dp", None),
    )
    out_specs = P(("grp", "dp"), None)
    return jax.shard_map(local, mesh=mesh, in_specs=in_specs, out_specs=out_specs, check_vma=False)
```

time: 186 us -> 150 us (0.81)
  blocking collectives: 98.4 us -> 11.2 us
  waiting for transfers between devices: 49.1 us -> 105 us
  matrix products: 24.4 us -> 15.9 us
  other arithmetic: 0.21 us -> 2.42 us
    psum x1 -> x0, blocking collectives: 98.4 us -> none  [local(): totals = lax.psum(jnp.concatenate([left, right], axis=1), 'dp')]
    reduce_scatter x0 -> x1, waiting for transfers between devices: none -> 64.3 us  [local(): lax.psum_scatter(jnp.concatenate([left, right], axis=1), 'dp', scatter_di...]
    all_to_all x0 -> x1, blocking collectives: none -> 11.2 us  [local(): return lax.all_to_all(part, 'dp', split_axis=0, concat_axis=1, tiled=True)]
    dot_general x2, matrix products: 11.1 us -> 2.58 us  [the longest x1 2.29 us: local(): lax.dot_general(every, queries, (((1,), (1,)), ((), ())), preferred_eleme...]
    all_gather x1, waiting for transfers between devices: 48.4 us -> 40.6 us  [local(): every = lax.all_gather(flat, 'dp', axis=0, tiled=True)]
  transfers between devices with their start and end apart: 1 -> 2, of which waited for: 1 -> 2; matrix products, arithmetic and copies ran while one was open for 8% -> 0% of each run, Pallas kernels for 0% -> 0%
where the time goes in v1:
time: 150 us
  waiting for transfers between devices  105 us (70%)
  matrix products  15.9 us (11%)
  between operations  13.5 us (9%)
  blocking collectives  11.2 us (7%)
  other arithmetic  2.42 us (2%)
  local copies, waits for them, and re-layouts  1.69 us (1%)
    reduce_scatter x1, waiting for transfers between devices, local(): lax.psum_scatter(jnp.concatenate([left, right], axis=1), 'dp', scatter_di...  64.3 us
    all_gather x1, waiting for transfers between devices, local(): every = lax.all_gather(flat, 'dp', axis=0, tiled=True)  40.6 us
    all_to_all x1, blocking collectives, local(): return lax.all_to_all(part, 'dp', split_axis=0, concat_axis=1, tiled=True)  11.2 us
    dot_general x1, matrix products, local(): right = jnp.dot(out_grads, out_basis, preferred_element_type=jnp.float32)  9.67 us
    dot_general x1, matrix products, local(): left = jnp.dot(inputs, in_basis, preferred_element_type=jnp.float32)  3.66 us
  transfers between devices with their start and end apart: 2, of which 2 were waited for; matrix products, arithmetic and copies ran while one was open for 0% of the time, Pallas kernels for 0%

profile of v1, /device:TPU:0, one launch (start us, length us, event | category | flops | bytes accessed | tf_op | source)
XLA Modules:
  0.0 149.7 jit_solution(8150759268334038420)
XLA Ops:
  6.5 0.0 copy-start
  6.5 0.0 copy-start.1
  6.5 0.0 reduce-scatter.2.cloned.1.call-start
  6.5 3.7 %fusion.5 = f32[4096,64]{0,1:T(8,128)S(1)} fusion(bf16[4096,512]{1,0:T(8,128)(2,1)} %param.7, bf16[512,64]{0,1:T(8,128)(2,1)} %param.9), kind=kOutput, calls=%fused_computation.13 | convolution fusion | flops 268435456 | bytes 5308416 | tf_op jit(solution)/shard_map/dot_general | solution.py:12
  10.2 0.0 copy-done.1
  10.2 9.7 %fusion.6 = f32[4096,64]{0,1:T(8,128)S(1)} fusion(bf16[4096,1792]{1,0:T(8,128)(2,1)} %param.8, bf16[1792,64]{0,1:T(8,128)(2,1)S(1)} %copy-done.1), kind=kOutput, calls=%fused_computation.14 | convolution fusion | flops 939524096 | bytes 15958016 | tf_op jit(solution)/shard_map/dot_general | solution.py:13
  19.9 0.0 copy-start.3
  19.9 0.0 copy-start.2
  19.9 1.5 pad_maximum_fusion
  21.4 0.0 reduce-scatter.2.cloned.1.call-update
  21.4 0.0 all-gather.2.cloned.1.call-start
  21.5 0.0 copy-done.3
  21.5 0.0 copy-done.2
  21.5 64.3 %reduce-scatter.2.cloned.1.call-done = f32[256,128]{0,1:T(8,128)} async-done(((f32[4096,128]{0,1:T(8,128)}), f32[256,128]{0,1:T(8,128)}) %reduce-scatter.2.cloned.1.call-update) | async-done | bytes 131088 | tf_op jit(solution)/shard_map/reduce_scatter | solution.py:14
  85.8 0.9 convert_element_type.24
  86.8 0.3 fusion.1
  87.1 0.1 copy.9
  87.1 0.9 convert_element_type.29
  88.1 0.0 all-gather.2.cloned.1.call-update
  88.1 40.6 %all-gather.2.cloned.1.call-done = bf16[256,4096]{1,0:T(8,128)(2,1)} async-done(((bf16[16,4096]{1,0:T(8,128)(2,1)}), bf16[256,4096]{1,0:T(8,128)(2,1)}) %all-gather.2.cloned.1.call-update) | async-done | bytes 2097168 | tf_op jit(solution)/shard_map/all_gather | solution.py:21
  128.7 0.0 copy-done
  128.7 2.3 %fusion.7 = f32[256,128]{1,0:T(8,128)S(1)} fusion(bf16[256,4096]{1,0:T(8,128)(2,1)} %all-gather.2.cloned.1.call-done, bf16[128,4096]{1,0:T(8,128)(2,1)S(1)} %copy-done), kind=kOutput, calls=%fused_computation.15 | convolution fusion | flops 268435456 | bytes 3276800 | tf_op jit(solution)/shard_map/dot_general | solution.py:22
  131.0 11.2 %all_to_all.19 = f32[16,16,128]{2,1,0:T(8,128)S(1)} all-to-all(f32[16,16,128]{2,1,0:T(8,128)S(1)} %bitcast.23), channel_id=1, replica_groups=mesh['grp'=2,'dp'=16] {'dp'}, dimensions={0} | all-to-all | bytes 262144 | tf_op jit(solution)/shard_map/all_to_all | solution.py:23
  142.2 0.7 copy_bitcast_fusion
  (3 shorter events, 0.0 us)
Async XLA Ops:
  6.5 122.1 %copy-start = (bf16[128,4096]{1,0:T(8,128)(2,1)S(1)}, bf16[128,4096]{1,0:T(8,128)(2,1)}, u32[]{:S(2)}) copy-start(bf16[128,4096]{1,0:T(8,128)(2,1)} %param.13) | copy-start | bytes 3145732
  6.5 3.7 %copy-start.1 = (bf16[1792,64]{0,1:T(8,128)(2,1)S(1)}, bf16[1792,64]{0,1:T(8,128)(2,1)}, u32[]{:S(2)}) copy-start(bf16[1792,64]{0,1:T(8,128)(2,1)} %param.10) | copy-start | bytes 688132
  6.5 79.3 %reduce-scatter.2.cloned.1.call-start = ((), (), s32[]{:S(2)}) async-start(), calls=%async_computation.2 | async-start | bytes 2228224 | tf_op jit(solution)/shard_map/reduce_scatter | solution.py:14
  19.9 1.6 %copy-start.3 = (s32[1,16]{1,0:T(1,128)S(1)}, s32[1,16]{1,0:T(1,128)}, u32[]{:S(2)}) copy-start(s32[1,16]{1,0:T(1,128)} %param.12) | copy-start | bytes 196
  19.9 1.6 %copy-start.2 = (s32[1,256]{1,0:T(1,128)S(1)}, s32[1,256]{1,0:T(1,128)}, u32[]{:S(2)}) copy-start(s32[1,256]{1,0:T(1,128)} %param.11) | copy-start | bytes 3076
  21.4 107.3 %all-gather.2.cloned.1.call-start = ((), (), s32[]{:S(2)}) async-start(), calls=%async_computation.3 | async-start | bytes 2228224 | tf_op jit(solution)/shard_map/all_gather | solution.py:21
Sparse Core Ops, SparseCore 0:
  21.5 64.2 reduce-scatter.1
  88.2 40.4 all-gather.1

commit v2 on v1

v2 whole, which is shorter than its diff:
```python
import functools

import jax
import jax.numpy as jnp
from jax import lax
from jax.experimental import pallas as pl
from jax.experimental.pallas import tpu as pltpu
from jax.sharding import PartitionSpec as P

MESH = pl.DeviceIdType.MESH
F32, BF16 = jnp.float32, jnp.bfloat16
NT = (((1,), (1,)), ((), ()))


def kernel(
    far, x_hbm, g_hbm, wi_ref, wo_ref, ids_ref, cnt_ref, q_hbm, out_ref,
    x_v, g_v, w_v, q_v, core_out, core_in, own, y_out, y_in, z_out, z_in, low, lhs, grads, s_out, s_in,
    x_sem, g_sem, q_sem, qs_sem, qr_sem, cs_sem, cr_sem, ys_sem, yr_sem, zs_sem, zr_sem,
    az_s, az_r, ay_s, ay_r, ss_sem, sr_sem,
):
    me = lax.axis_index("dp")
    z, y, c = me // 4, (me // 2) % 2, me % 2
    chip = me // 2
    rows = ids_ref.shape[1]
    examples = cnt_ref.shape[1]
    rank = wi_ref.shape[1]
    feats = wi_ref.shape[0]
    group = 4 * rows
    nq = q_hbm.shape[0]

    def device(zz, yy, cc):
        return {"dp": zz * 4 + yy * 2 + cc}

    def send(src, dst, ssem, rsem, target):
        copy = pltpu.make_async_remote_copy(
            src_ref=src, dst_ref=dst, send_sem=ssem, recv_sem=rsem, device_id=target, device_id_type=MESH)
        copy.start()
        return copy

    zs = [lax.rem(z + 1 + s, far) for s in range(far)]
    loads = []
    for s in range(far):
        at = pl.ds(pl.multiple_of(zs[s] * group, group), group)
        a = pltpu.make_async_copy(x_hbm.at[at, :], x_v.at[s], x_sem.at[s])
        b = pltpu.make_async_copy(g_hbm.at[at, :], g_v.at[s], g_sem.at[s])
        a.start()
        b.start()
        loads.append((a, b))

    barrier = pltpu.get_barrier_semaphore()
    pl.semaphore_signal(barrier, inc=1, device_id=device(z, y, 1 - c), device_id_type=MESH)
    for dz in range(far):
        for dy in range(2):
            if dz or dy:
                yy = 1 - y if dy else y
                pl.semaphore_signal(
                    barrier, inc=1, device_id=device(lax.rem(z + dz, far), yy, c), device_id_type=MESH)

    w_v[:feats, :] = jnp.concatenate([wi_ref[...], jnp.zeros_like(wi_ref)], axis=1)
    w_v[feats:, :] = jnp.concatenate([jnp.zeros_like(wo_ref), wo_ref[...]], axis=1)
    labels = lax.broadcasted_iota(jnp.int32, (examples, rows), 0)
    onehot = jnp.where(labels == ids_ref[...], 1.0, 0.0).astype(F32)
    low[0, 0, 2 * rank:, :] = onehot.astype(BF16)

    pl.semaphore_wait(barrier, 2 * far)

    q_rows = pl.ds(pl.multiple_of(c * nq, nq), nq)
    q_far = None
    q_near = None

    def project(s, yy, cc):
        at = pl.ds(pl.multiple_of((yy * 2 + cc) * rows, rows), rows)
        return (jnp.dot(x_v[s, at, :], w_v[:feats, :], preferred_element_type=F32)
                + jnp.dot(g_v[s, at, :], w_v[feats:, :], preferred_element_type=F32))

    core_copies, y_copies, z_copies = [], [], []

    def z_stage(s):
        core_copies[2 * s + 1].wait_recv()
        y_copies[s].wait_recv()
        total = own[2 * s + 1] + core_in[2 * s + 1] + y_in[s].astype(F32)
        if s == far - 1:
            return total
        z_out[s] = total.astype(BF16)
        z_copies.append(send(z_out.at[s], z_in.at[s], zs_sem.at[s], zr_sem.at[s], device(zs[s], y, c)))

    for s in range(far):
        loads[s][0].wait()
        loads[s][1].wait()
        for k, yy in enumerate((1 - y, y)):
            core_out[2 * s + k] = project(s, yy, 1 - c)
            core_copies.append(send(core_out.at[2 * s + k], core_in.at[2 * s + k], cs_sem.at[2 * s + k],
                                    cr_sem.at[2 * s + k], device(z, y, 1 - c)))
        for k, yy in enumerate((1 - y, y)):
            own[2 * s + k] = project(s, yy, c)
        core_copies[2 * s].wait_recv()
        y_out[s] = (own[2 * s] + core_in[2 * s]).astype(BF16)
        y_copies.append(send(y_out.at[s], y_in.at[s], ys_sem.at[s], yr_sem.at[s], device(z, 1 - y, c)))
        if s:
            z_stage(s - 1)
    q_far = send(q_hbm, q_v.at[q_rows, :], qs_sem, qr_sem, device(z, y, 1 - c))
    q_near = pltpu.make_async_copy(q_hbm, q_v.at[q_rows, :], q_sem)
    q_near.start()
    total = z_stage(far - 1)
    for s in range(far - 1):
        z_copies[s].wait_recv()
        total = total + z_in[s].astype(F32)
    low[0, 0, :2 * rank, :] = total.T.astype(BF16)

    gz = [None] * far
    gy = [None] * far
    for dz in range(1, far):
        gz[dz] = send(low.at[0, 0], low.at[dz, 0], az_s.at[dz], az_r.at[dz], device(lax.rem(z + dz, far), y, c))
    gy[0] = send(low.at[0, 0], low.at[0, 1], ay_s.at[0], ay_r.at[0], device(z, 1 - y, c))

    def outer(dz, dy):
        left = low[dz, dy, :rank, :].astype(F32)
        right = low[dz, dy, rank:2 * rank, :]
        hot = low[dz, dy, 2 * rank:, :].astype(F32)
        for i in range(rank):
            lhs[(i // 2) * examples:(i // 2 + 1) * examples, (i % 2) * rows:(i % 2 + 1) * rows] = (
                hot * left[i:i + 1, :]).astype(BF16)
        none = jnp.zeros_like(right)
        rhs = jnp.concatenate(
            [jnp.concatenate([right, none], axis=1), jnp.concatenate([none, right], axis=1)], axis=0)
        flat = lax.dot_general(lhs[...], rhs, NT, preferred_element_type=F32).astype(BF16)
        r = 2 * dz + dy
        for i in range(rank // 2):
            grads[r * examples:(r + 1) * examples, i * 2 * rank:(i + 1) * 2 * rank] = (
                flat[i * examples:(i + 1) * examples, :])

    outer(0, 0)
    for dz in range(1, far):
        gz[dz].wait_recv()
        gy[dz] = send(low.at[dz, 0], low.at[dz, 1], ay_s.at[dz], ay_r.at[dz], device(z, 1 - y, c))
        outer(dz, 0)
    for dz in range(far):
        gy[dz].wait_recv()
        outer(dz, 1)

    q_near.wait()
    q_far.wait_recv()
    scores = lax.dot_general(grads[...], q_v[...], NT, preferred_element_type=F32)
    back = []
    for dz in range(far):
        for dy in range(2):
            r = 2 * dz + dy
            block = scores[r * examples:(r + 1) * examples, :]
            if r == 0:
                s_in[chip] = block
            else:
                s_out[r] = block
                yy = 1 - y if dy else y
                back.append(send(s_out.at[r], s_in.at[chip], ss_sem.at[r], sr_sem.at[r],
                                 device(lax.rem(z - dz + far, far), yy, c)))
    diag = lax.broadcasted_iota(jnp.int32, (examples, examples), 0) == lax.broadcasted_iota(
        jnp.int32, (examples, examples), 1)
    counts = jnp.sum(jnp.where(diag, jnp.broadcast_to(cnt_ref[...].astype(F32), (examples, examples)), 0.0),
                     axis=1, keepdims=True)
    for copy in back:
        copy.wait_recv()
    for k in range(2 * far):
        out_ref[:, k * 2 * nq:(k + 1) * 2 * nq] = s_in[k] / counts
    for copy in core_copies + y_copies + z_copies + gz[1:] + gy + back + [q_far]:
        copy.wait_send()


def local(inputs, out_grads, in_basis, out_basis, example_ids, loss_counts, queries):
    rows = example_ids.shape[1]
    examples = loss_counts.shape[1]
    rank = in_basis.shape[1]
    n = inputs.shape[0] // rows
    far = n // 4
    nq, flat = queries.shape
    wide = 2 * rank
    vmem, hbm = pl.BlockSpec(memory_space=pltpu.VMEM), pl.BlockSpec(memory_space=pl.ANY)
    dma = pltpu.SemaphoreType.DMA
    feats = in_basis.shape[0] + out_basis.shape[0]
    return pl.pallas_call(
        functools.partial(kernel, far),
        out_shape=jax.ShapeDtypeStruct((examples, n * nq), F32),
        in_specs=[hbm, hbm, vmem, vmem, vmem, vmem, hbm],
        out_specs=vmem,
        scratch_shapes=[
            pltpu.VMEM((far, 4 * rows, inputs.shape[1]), BF16),
            pltpu.VMEM((far, 4 * rows, out_grads.shape[1]), BF16),
            pltpu.VMEM((feats, wide), BF16),
            pltpu.VMEM((2 * nq, flat), BF16),
            pltpu.VMEM((2 * far, rows, wide), F32),
            pltpu.VMEM((2 * far, rows, wide), F32),
            pltpu.VMEM((2 * far, rows, wide), F32),
            pltpu.VMEM((far, rows, wide), BF16),
            pltpu.VMEM((far, rows, wide), BF16),
            pltpu.VMEM((far, rows, wide), BF16),
            pltpu.VMEM((far, rows, wide), BF16),
            pltpu.VMEM((far, 2, wide + examples, rows), BF16),
            pltpu.VMEM((rank // 2 * examples, 2 * rows), BF16),
            pltpu.VMEM((2 * far * examples, flat), BF16),
            pltpu.VMEM((2 * far, examples, 2 * nq), F32),
            pltpu.VMEM((2 * far, examples, 2 * nq), F32),
            dma((far,)), dma((far,)), dma, dma, dma,
            dma((2 * far,)), dma((2 * far,)), dma((far,)), dma((far,)), dma((far,)), dma((far,)),
            dma((far,)), dma((far,)), dma((far,)), dma((far,)), dma((2 * far,)), dma((2 * far,)),
        ],
        compiler_params=pltpu.CompilerParams(
            collective_id=0, has_side_effects=True, vmem_limit_bytes=56 * 2 ** 20),
        cost_estimate=pl.CostEstimate(
            flops=2 * n * rows * feats * wide, bytes_accessed=2 * n * rows * feats, transcendentals=0),
    )(inputs, out_grads, in_basis, out_basis, example_ids, loss_counts, queries)


def solution(mesh):
    in_specs = (
        P("grp", "dp"),
        P("grp", "dp"),
        P("dp", None),
        P("dp", None),
        P(("grp", "dp"), None),
        P(("grp", "dp"), None),
        P("dp", None),
    )
    out_specs = P(("grp", "dp"), None)
    return jax.shard_map(local, mesh=mesh, in_specs=in_specs, out_specs=out_specs, check_vma=False)
```

time: 150 us -> 46.5 us (0.31)
  waiting for transfers between devices: 105 us -> 0 us
  Pallas kernels: 0 us -> 41.2 us
  matrix products: 15.9 us -> 0 us
  between operations: 13.5 us -> 0.01 us
  blocking collectives: 11.2 us -> 0 us
  local copies, waits for them, and re-layouts: 1.69 us -> 5.08 us
  other arithmetic: 2.42 us -> 0 us
    reduce_scatter x1 -> x0, waiting for transfers between devices: 64.3 us -> none  [local(): lax.psum_scatter(jnp.concatenate([left, right], axis=1), 'dp', scatter_di...]
    pallas_call x0 -> x1, Pallas kernels: none -> 41.2 us  [local(): pl.pallas_call(functools.partial(kernel, far), out_shape=jax.ShapeDtypeSt...]
    all_gather x1 -> x0, waiting for transfers between devices: 40.6 us -> none  [local(): every = lax.all_gather(flat, 'dp', axis=0, tiled=True)]
    dot_general x4 -> x0, matrix products: 15.9 us -> none  [the longest x1 9.67 us: local(): right = jnp.dot(out_grads, out_basis, preferred_element_type=jnp.float32)]
    all_to_all x1 -> x0, blocking collectives: 11.2 us -> none  [local(): return lax.all_to_all(part, 'dp', split_axis=0, concat_axis=1, tiled=True)]
    unnamed x8 -> x3, local copies, waits for them, and re-layouts: 0.02 us -> 5.08 us
  transfers between devices with their start and end apart: 2 -> 0, of which waited for: 2 -> 0; matrix products, arithmetic and copies ran while one was open for 0% -> 0% of each run, Pallas kernels for 0% -> 0%
where the time goes in v2:
time: 46.5 us; the launch traced here: 46.3 us
  Pallas kernels  41.2 us (89%)
  local copies, waits for them, and re-layouts  5.08 us (11%)
    pallas_call x1, Pallas kernels, local(): pl.pallas_call(functools.partial(kernel, far), out_shape=jax.ShapeDtypeSt...  41.2 us
    unnamed x3, local copies, waits for them, and re-layouts  5.08 us

profile of v2, /device:TPU:0, one launch (start us, length us, event | category | flops | bytes accessed | tf_op | source)
XLA Modules:
  0.0 46.3 jit_solution(7968216866905502699)
XLA Ops:
  0.0 1.6 %copy.8.wi_ref = bf16[512,64]{1,0:T(8,128)(2,1)} copy(bf16[512,64]{0,1:T(8,128)(2,1)} %param.9) | data formatting | bytes 131072 | tf_op args[2]
  1.6 1.9 %copy.9.wo_ref = bf16[1792,64]{1,0:T(8,128)(2,1)} copy(bf16[1792,64]{0,1:T(8,128)(2,1)} %param.10) | data formatting | bytes 458752 | tf_op args[3]
  3.5 41.2 %shard_map.73 = f32[16,2048]{1,0:T(8,128)} custom-call(bf16[4096,512]{1,0:T(8,128)(2,1)} %x_hbm.1, bf16[4096,1792]{1,0:T(8,128)(2,1)} %g_hbm.1, bf16[512,64]{1,0:T(8,128)(2,1)} %copy.8.wi_ref, bf16[1792,64]{1,0:T(8,128)(2,1)} %copy.9.wo_ref, s32[1,256]{1,0:T(1,128)} %ids_ref.1, s32[1,16]{1,0:T(1,128)} %cnt_ref.1, bf16[128,4096]{1,0:T(8,128)(2,1)} %q_hbm.1), custom_call_target="tpu_custom_call" | custom-call | flops 2415919104 | bytes 18874368 | tf_op jit(solution)/shard_map/pallas_call | solution.py:179
  44.8 1.6 %copy.11 = f32[16,2048]{1,0:T(8,128)} copy(f32[16,2048]{1,0:T(8,128)} %shard_map.73) | data formatting | bytes 262144

commit v3 on v2

--- a/solution.py
+++ b/solution.py
@@ -13,9 +13,9 @@
 
 
 def kernel(
-    far, x_hbm, g_hbm, wi_ref, wo_ref, ids_ref, cnt_ref, q_hbm, out_ref,
+    far, x_hbm, g_hbm, wi_hbm, wo_hbm, ids_ref, cnt_ref, q_hbm, out_ref,
     x_v, g_v, w_v, q_v, core_out, core_in, own, y_out, y_in, z_out, z_in, low, lhs, grads, s_out, s_in,
-    x_sem, g_sem, q_sem, qs_sem, qr_sem, cs_sem, cr_sem, ys_sem, yr_sem, zs_sem, zr_sem,
+    x_sem, g_sem, w_sem, q_sem, qs_sem, qr_sem, cs_sem, cr_sem, ys_sem, yr_sem, zs_sem, zr_sem,
     az_s, az_r, ay_s, ay_r, ss_sem, sr_sem,
 ):
     me = lax.axis_index("dp")
@@ -23,8 +23,7 @@
     chip = me // 2
     rows = ids_ref.shape[1]
     examples = cnt_ref.shape[1]
-    rank = wi_ref.shape[1]
-    feats = wi_ref.shape[0]
+    rank, feats = wi_hbm.shape
     group = 4 * rows
     nq = q_hbm.shape[0]
 
@@ -37,6 +36,13 @@
         copy.start()
         return copy
 
+    w_v[...] = jnp.zeros_like(w_v)
+    w_copies = [
+        pltpu.make_async_copy(wi_hbm, w_v.at[:rank, :feats], w_sem.at[0]),
+        pltpu.make_async_copy(wo_hbm, w_v.at[rank:, feats:], w_sem.at[1]),
+    ]
+    for copy in w_copies:
+        copy.start()
     zs = [lax.rem(z + 1 + s, far) for s in range(far)]
     loads = []
     for s in range(far):
@@ -56,8 +62,6 @@
                 pl.semaphore_signal(
                     barrier, inc=1, device_id=device(lax.rem(z + dz, far), yy, c), device_id_type=MESH)
 
-    w_v[:feats, :] = jnp.concatenate([wi_ref[...], jnp.zeros_like(wi_ref)], axis=1)
-    w_v[feats:, :] = jnp.concatenate([jnp.zeros_like(wo_ref), wo_ref[...]], axis=1)
     labels = lax.broadcasted_iota(jnp.int32, (examples, rows), 0)
     onehot = jnp.where(labels == ids_ref[...], 1.0, 0.0).astype(F32)
     low[0, 0, 2 * rank:, :] = onehot.astype(BF16)
@@ -70,8 +74,8 @@
 
     def project(s, yy, cc):
         at = pl.ds(pl.multiple_of((yy * 2 + cc) * rows, rows), rows)
-        return (jnp.dot(x_v[s, at, :], w_v[:feats, :], preferred_element_type=F32)
-                + jnp.dot(g_v[s, at, :], w_v[feats:, :], preferred_element_type=F32))
+        return (lax.dot_general(x_v[s, at, :], w_v[:, :feats], NT, preferred_element_type=F32)
+                + lax.dot_general(g_v[s, at, :], w_v[:, feats:], NT, preferred_element_type=F32))
 
     core_copies, y_copies, z_copies = [], [], []
 
@@ -84,6 +88,8 @@
         z_out[s] = total.astype(BF16)
         z_copies.append(send(z_out.at[s], z_in.at[s], zs_sem.at[s], zr_sem.at[s], device(zs[s], y, c)))
 
+    for copy in w_copies:
+        copy.wait()
     for s in range(far):
         loads[s][0].wait()
         loads[s][1].wait()
@@ -124,35 +130,39 @@
         rhs = jnp.concatenate(
             [jnp.concatenate([right, none], axis=1), jnp.concatenate([none, right], axis=1)], axis=0)
         flat = lax.dot_general(lhs[...], rhs, NT, preferred_element_type=F32).astype(BF16)
-        r = 2 * dz + dy
+        r = dy * far + dz
         for i in range(rank // 2):
             grads[r * examples:(r + 1) * examples, i * 2 * rank:(i + 1) * 2 * rank] = (
                 flat[i * examples:(i + 1) * examples, :])
+
+    back = []
+
+    def score(dy):
+        half = slice(dy * far * examples, (dy + 1) * far * examples)
+        scores = lax.dot_general(grads[half, :], q_v[...], NT, preferred_element_type=F32)
+        yy = 1 - y if dy else y
+        for dz in range(far):
+            r = dy * far + dz
+            part = scores[dz * examples:(dz + 1) * examples, :]
+            if r == 0:
+                s_in[chip] = part
+            else:
+                s_out[r] = part
+                back.append(send(s_out.at[r], s_in.at[chip], ss_sem.at[r], sr_sem.at[r],
+                                 device(lax.rem(z - dz + far, far), yy, c)))
 
     outer(0, 0)
     for dz in range(1, far):
         gz[dz].wait_recv()
         gy[dz] = send(low.at[dz, 0], low.at[dz, 1], ay_s.at[dz], ay_r.at[dz], device(z, 1 - y, c))
         outer(dz, 0)
+    q_near.wait()
+    q_far.wait_recv()
+    score(0)
     for dz in range(far):
         gy[dz].wait_recv()
         outer(dz, 1)
-
-    q_near.wait()
-    q_far.wait_recv()
-    scores = lax.dot_general(grads[...], q_v[...], NT, preferred_element_type=F32)
-    back = []
-    for dz in range(far):
-        for dy in range(2):
-            r = 2 * dz + dy
-            block = scores[r * examples:(r + 1) * examples, :]
-            if r == 0:
-                s_in[chip] = block
-            else:
-                s_out[r] = block
-                yy = 1 - y if dy else y
-                back.append(send(s_out.at[r], s_in.at[chip], ss_sem.at[r], sr_sem.at[r],
-                                 device(lax.rem(z - dz + far, far), yy, c)))
+    score(1)
     diag = lax.broadcasted_iota(jnp.int32, (examples, examples), 0) == lax.broadcasted_iota(
         jnp.int32, (examples, examples), 1)
     counts = jnp.sum(jnp.where(diag, jnp.broadcast_to(cnt_ref[...].astype(F32), (examples, examples)), 0.0),
@@ -179,12 +189,12 @@
     return pl.pallas_call(
         functools.partial(kernel, far),
         out_shape=jax.ShapeDtypeStruct((examples, n * nq), F32),
-        in_specs=[hbm, hbm, vmem, vmem, vmem, vmem, hbm],
+        in_specs=[hbm, hbm, hbm, hbm, vmem, vmem, hbm],
         out_specs=vmem,
         scratch_shapes=[
             pltpu.VMEM((far, 4 * rows, inputs.shape[1]), BF16),
             pltpu.VMEM((far, 4 * rows, out_grads.shape[1]), BF16),
-            pltpu.VMEM((feats, wide), BF16),
+            pltpu.VMEM((wide, feats), BF16),
             pltpu.VMEM((2 * nq, flat), BF16),
             pltpu.VMEM((2 * far, rows, wide), F32),
             pltpu.VMEM((2 * far, rows, wide), F32),
@@ -198,7 +208,7 @@
             pltpu.VMEM((2 * far * examples, flat), BF16),
             pltpu.VMEM((2 * far, examples, 2 * nq), F32),
             pltpu.VMEM((2 * far, examples, 2 * nq), F32),
-            dma((far,)), dma((far,)), dma, dma, dma,
+            dma((far,)), dma((far,)), dma((2,)), dma, dma, dma,
             dma((2 * far,)), dma((2 * far,)), dma((far,)), dma((far,)), dma((far,)), dma((far,)),
             dma((far,)), dma((far,)), dma((far,)), dma((far,)), dma((2 * far,)), dma((2 * far,)),
         ],
@@ -206,7 +216,7 @@
             collective_id=0, has_side_effects=True, vmem_limit_bytes=56 * 2 ** 20),
         cost_estimate=pl.CostEstimate(
             flops=2 * n * rows * feats * wide, bytes_accessed=2 * n * rows * feats, transcendentals=0),
-    )(inputs, out_grads, in_basis, out_basis, example_ids, loss_counts, queries)
+    )(inputs, out_grads, in_basis.T, out_basis.T, example_ids, loss_counts, queries)
 
 
 def solution(mesh):

time: 46.5 us -> 45 us (0.968)
  local copies, waits for them, and re-layouts: 5.08 us -> 1.57 us
  Pallas kernels: 41.2 us -> 43.2 us
    unnamed x3 -> x1, local copies, waits for them, and re-layouts: 5.08 us -> 1.57 us
    pallas_call x1, Pallas kernels: 41.2 us -> 43.2 us  [local(): pl.pallas_call(functools.partial(kernel, far), out_shape=jax.ShapeDtypeSt...]
where the time goes in v3:
time: 45 us; the launch traced here: 44.8 us
  Pallas kernels  43.2 us (96%)
  local copies, waits for them, and re-layouts  1.57 us (3%)
    pallas_call x1, Pallas kernels, local(): pl.pallas_call(functools.partial(kernel, far), out_shape=jax.ShapeDtypeSt...  43.2 us
    unnamed x1, local copies, waits for them, and re-layouts  1.57 us

profile of v3, /device:TPU:0, one launch (start us, length us, event | category | flops | bytes accessed | tf_op | source)
XLA Modules:
  0.0 44.8 jit_solution(16101229519470291329)
XLA Ops:
  0.0 43.2 %shard_map.73 = f32[16,2048]{1,0:T(8,128)} custom-call(bf16[4096,512]{1,0:T(8,128)(2,1)} %x_hbm.1, bf16[4096,1792]{1,0:T(8,128)(2,1)} %g_hbm.1, bf16[64,512]{1,0:T(8,128)(2,1)} %bitcast.3, bf16[64,1792]{1,0:T(8,128)(2,1)} %bitcast.2, s32[1,256]{1,0:T(1,128)} %ids_ref.1, s32[1,16]{1,0:T(1,128)} %cnt_ref.1, bf16[128,4096]{1,0:T(8,128)(2,1)} %q_hbm.1), custom_call_target="tpu_custom_call" | custom-call | flops 2415919104 | bytes 18874368 | tf_op jit(solution)/shard_map/pallas_call | solution.py:189
  43.2 1.6 %copy.9 = f32[16,2048]{1,0:T(8,128)} copy(f32[16,2048]{1,0:T(8,128)} %shard_map.73) | data formatting | bytes 262144
